TPU v7x, 32 devices: a whole 2x2x4 slice. The times are simulated.
32 devices in a mesh: vocab: 4 (over y, core), dp: 4 (over z), teacher: 2 (over x).
Axes of the slice: x: 2, y: 2, z: 4, core: 2. Of those that a mesh axis runs over, the one named last changes fastest.
Arguments:
- hidden_states: bfloat16 [2048, 4096], P('teacher'), may hold values from -300 to 300
- head_weight: bfloat16 [4096, 16384], P(None, ('vocab', 'dp')), may hold values from -3 to 3
- teacher_logits: bfloat16 [2048, 16384], P(None, ('vocab', 'dp', 'teacher')), may hold values from -20 to 460
- token_weight: float32 [2048], P('teacher'), may hold values from 2 to 20
Outputs:
- hidden_grad: bfloat16 [2048, 4096], P('teacher', ('vocab', 'dp'))
- weight_grad: bfloat16 [4096, 16384], P('teacher', ('vocab', 'dp'))
All inputs are finite; a program needn't handle non-finite values.
Results may differ from a plain program's by a relative error of at most 0.005.
Values may be sent and summed in bfloat16 or wider, within the bound.
A program may use at most 192 MiB of HBM per device.

v0:
```python
import jax
import jax.numpy as jnp
from jax import lax
from jax.sharding import PartitionSpec as P

D = 4096


def per_device(hidden_states, head_weight, teacher_logits, token_weight):
    teacher = lax.all_to_all(
        teacher_logits, "teacher", split_axis=0, concat_axis=1, tiled=True
    ).astype(jnp.float32)
    logits = jnp.dot(hidden_states, head_weight, preferred_element_type=jnp.float32)
    student_top = jnp.max(logits, axis=1)
    teacher_top = jnp.max(teacher, axis=1)
    student_top, teacher_top = lax.pmax((student_top, teacher_top), ("vocab", "dp"))
    student_total = jnp.sum(jnp.exp(logits - student_top[:, None]), axis=1)
    teacher_total = jnp.sum(jnp.exp(teacher - teacher_top[:, None]), axis=1)
    student_total, teacher_total = lax.psum((student_total, teacher_total), ("vocab", "dp"))
    student_norm = student_top + jnp.log(student_total)
    teacher_norm = teacher_top + jnp.log(teacher_total)
    logit_grad = (
        token_weight[:, None]
        * (jnp.exp(logits - student_norm[:, None]) - jnp.exp(teacher - teacher_norm[:, None]))
    ).astype(jnp.bfloat16)
    hidden_share = lax.psum_scatter(
        lax.dot_general(
            head_weight, logit_grad, (((1,), (1,)), ((), ())), preferred_element_type=jnp.float32
        ),
        ("vocab", "dp"),
        scatter_dimension=0,
        tiled=True,
    )
    hidden_grad = hidden_share.T.astype(jnp.bfloat16)
    share_width = D // lax.axis_size("teacher")
    own_offset = lax.axis_index("teacher") * share_width
    state_cols = lax.dynamic_slice_in_dim(
        lax.all_gather(hidden_states, "teacher", axis=0, tiled=True), own_offset, share_width, 1
    )
    weight_share = lax.dot_general(
        state_cols,
        lax.all_gather(logit_grad, "teacher", axis=0, tiled=True),
        (((0,), (0,)), ((), ())),
        preferred_element_type=jnp.float32,
    )
    return (hidden_grad, weight_share.astype(jnp.bfloat16))


def solution(mesh):
    return jax.shard_map(
        per_device,
        mesh=mesh,
        in_specs=(
            P("teacher", None),
            P(None, ("vocab", "dp")),
            P(None, ("vocab", "dp", "teacher")),
            P("teacher"),
        ),
        out_specs=(P("teacher", ("vocab", "dp")), P("teacher", ("vocab", "dp"))),
        check_vma=False,
    )
```

profile of v0, /device:TPU:0, one launch (start us, length us, event | category | flops | bytes accessed | tf_op | source)
XLA Modules:
  0.0 393.9 jit_solution(17715888473232478544)
XLA Ops:
  8.0 4.0 %copy.6 = bf16[2,1024,512]{1,2,0:T(8,128)(2,1)} copy(bf16[2,1024,512]{2,1,0:T(8,128)(2,1)} %bitcast.22) | data formatting | bytes 4194304 | tf_op jit(solution)/shard_map/all_to_all | solution.py:10
  12.0 4.2 %all-to-all-start = ((bf16[2,1024,512]{1,2,0:T(8,128)(2,1)}), bf16[2,1024,512]{1,2,0:T(8,128)(2,1)S(1)}, u32[]{:S(2)}, u32[]{:S(2)}) async-start(bf16[2,1024,512]{1,2,0:T(8,128)(2,1)} %copy.6), calls=%async_computation | async-start | bytes 4194304 | tf_op jit(solution)/shard_map/all_to_all | solution.py:10
  16.2 0.0 all-gather.5.cloned.1.call-start
  16.2 15.1 %fusion.10 = (f32[1024]{0:T(1024)S(1)}, f32[1024,1024]{0,1:T(8,128)}) fusion(bf16[1024,4096]{1,0:T(8,128)(2,1)} %param.4, bf16[4096,1024]{1,0:T(8,128)(2,1)} %param.5), kind=kOutput, calls=%fused_computation.15 | convolution fusion | flops 8590982144 | bytes 20975616 | tf_op jit(solution)/shard_map/dot_general | solution.py:13
  31.3 10.8 %all-to-all-done = bf16[2,1024,512]{1,2,0:T(8,128)(2,1)S(1)} async-done(((bf16[2,1024,512]{1,2,0:T(8,128)(2,1)}), bf16[2,1024,512]{1,2,0:T(8,128)(2,1)S(1)}, u32[]{:S(2)}, u32[]{:S(2)}) %all-to-all-start) | async-done | bytes 2097184 | tf_op jit(solution)/shard_map/all_to_all | solution.py:10
  42.0 0.4 reduce_max.24
  42.4 33.9 %all-reduce.1 = (f32[1024]{0:T(1024)S(1)}, f32[1024]{0:T(1024)S(1)}) all-reduce(bf16[1024]{0:T(1024)(128)(2,1)S(1)} %reduce_max.24, f32[1024]{0:T(1024)S(1)} %get-tuple-element.6), channel_id=1, replica_groups=mesh['vocab'=4,'dp'=4,'teacher'=2] {'vocab','dp'}, use_global_device_ids=true, to_apply=%region_5.0 | all-reduce | flops 2048 | bytes 14336 | tf_op jit(solution)/shard_map/pmax | solution.py:16
  76.3 2.8 exponential_reduce_fusion.1
  79.1 0.7 exponential_reduce_fusion
  79.9 30.4 %all-reduce = (f32[1024]{0:T(1024)S(1)}, f32[1024]{0:T(1024)S(1)}) all-reduce(f32[1024]{0:T(1024)S(1)} %exponential_reduce_fusion, f32[1024]{0:T(1024)S(1)} %exponential_reduce_fusion.1), channel_id=1, replica_groups=mesh['vocab'=4,'dp'=4,'teacher'=2] {'vocab','dp'}, use_global_device_ids=true, to_apply=%region_7.0 | all-reduce | flops 2048 | bytes 16384 | tf_op jit(solution)/shard_map/psum | solution.py:19
  110.3 0.0 copy-done.1
  110.3 4.8 %fusion.5 = bf16[1024,1024]{0,1:T(8,128)(2,1)} fusion(f32[1024,1024]{0,1:T(8,128)} %get-tuple-element.7, f32[1024]{0:T(1024)S(1)} %get-tuple-element.8, f32[1024]{0:T(1024)S(1)} %get-tuple-element.9, f32[1024]{0:T(1024)S(1)} %copy-done.1, bf16[2,1024,512]{1,2,0:T(8,128)(2,1)S(1)} %all-to-all-done), kind=kLoop, calls=%fused_computation.7 | loop fusion | flops 6291456 | bytes 8400896 | tf_op jit(solution)/shard_map/convert_element_type | solution.py:25
  115.1 0.0 all-gather.5.cloned.1.call-update
  115.1 0.0 copy-start
  115.1 0.0 all-gather.3.cloned.1.call-start
  115.2 0.7 all-gather.3.cloned.1.call-update
  115.9 0.2 reduce-scatter.2.cloned.1.call-start
  116.1 0.6 copy-done
  116.7 14.5 %convolution_bitcast_fusion = f32[4096,1024]{0,1:T(8,128)} fusion(bf16[1024,1024]{0,1:T(8,128)(2,1)S(1)} %copy-done, bf16[4096,1024]{1,0:T(8,128)(2,1)} %param.5), kind=kOutput, calls=%fused_computation | convolution fusion | flops 8589934592 | bytes 27262976 | tf_op jit(solution)/shard_map/dot_general | solution.py:27
  131.2 0.0 reduce-scatter.2.cloned.1.call-update
  131.2 38.7 %all-gather.5.cloned.1.call-done = bf16[2048,1024]{0,1:T(8,128)(2,1)} async-done(((bf16[1024,1024]{0,1:T(8,128)(2,1)}), bf16[2048,1024]{0,1:T(8,128)(2,1)}) %all-gather.5.cloned.1.call-update) | async-done | bytes 4194320 | tf_op jit(solution)/shard_map/all_gather | solution.py:42
  170.0 200.5 %all-gather.3.cloned.1.call-done = bf16[2048,4096]{1,0:T(8,128)(2,1)} async-done(((bf16[1024,4096]{1,0:T(8,128)(2,1)}), bf16[2048,4096]{1,0:T(8,128)(2,1)}) %all-gather.3.cloned.1.call-update) | async-done | bytes 16777232 | tf_op jit(solution)/shard_map/all_gather | solution.py:38
  370.5 13.9 %fusion.6 = bf16[2048,1024]{1,0:T(8,128)(2,1)} fusion(bf16[2048,1024]{0,1:T(8,128)(2,1)} %all-gather.5.cloned.1.call-done, bf16[2048,4096]{1,0:T(8,128)(2,1)} %all-gather.3.cloned.1.call-done, s32[]{:T(128)S(6)} %select_n.3), kind=kOutput, calls=%fused_computation.10 | convolution fusion | flops 8592031744 | bytes 16777220 | tf_op jit(solution)/shard_map/dot_general | solution.py:40
  384.4 2.1 convert_bitcast_fusion
  (3 shorter events, 0.0 us)
Async XLA Ops:
  12.0 30.1 %all-to-all-start = ((bf16[2,1024,512]{1,2,0:T(8,128)(2,1)}), bf16[2,1024,512]{1,2,0:T(8,128)(2,1)S(1)}, u32[]{:S(2)}, u32[]{:S(2)}) async-start(bf16[2,1024,512]{1,2,0:T(8,128)(2,1)} %copy.6), calls=%async_computation | async-start | bytes 4194304 | tf_op jit(solution)/shard_map/all_to_all | solution.py:10
  16.2 153.8 %all-gather.5.cloned.1.call-start = ((), (), s32[]{:S(2)}) async-start(), calls=%async_computation.4 | async-start | bytes 6291456 | tf_op jit(solution)/shard_map/all_gather | solution.py:42
  31.3 79.0 %copy-start.1 = (f32[1024]{0:T(1024)S(1)}, f32[1024]{0:T(1024)}, u32[]{:S(2)}) copy-start(f32[1024]{0:T(1024)} %param.7) | copy-start | bytes 12292
  115.1 1.6 copy-start
  115.1 255.3 %all-gather.3.cloned.1.call-start = ((), (), s32[]{:S(2)}) async-start(), calls=%async_computation.3 | async-start | bytes 25165824 | tf_op jit(solution)/shard_map/all_gather | solution.py:38
  115.9 268.5 %reduce-scatter.2.cloned.1.call-start = ((), (), s32[]{:S(2)}) async-start(), calls=%async_computation.2 | async-start | bytes 17825792 | tf_op jit(solution)/shard_map/reduce_scatter | solution.py:26
Sparse Core Ops, SparseCore 0:
  115.2 54.6 all-gather.4
  171.5 198.8 all-gather.2
Sparse Core Ops, SparseCore 1:
  131.3 174.6 reduce-scatter.1
where the time goes:
time: 394 us
  waiting for transfers between devices  251 us (64%)
  blocking collectives  64.3 us (16%)
  matrix products  43.5 us (11%)
  between operations  15.5 us (4%)
  other arithmetic  10.8 us (3%)
  local copies, waits for them, and re-layouts  4.58 us (1%)
  starting transfers between devices  4.47 us (1%)
    all_gather x1, waiting for transfers between devices, per_device(): lax.all_gather(hidden_states, 'teacher', axis=0, tiled=True)  200 us
    all_gather x1, waiting for transfers between devices, per_device(): lax.all_gather(logit_grad, 'teacher', axis=0, tiled=True)  38.7 us
    pmax x1, blocking collectives, per_device(): lax.pmax((student_top, teacher_top), ('vocab', 'dp'))  33.9 us
    psum x1, blocking collectives, per_device(): lax.psum((student_total, teacher_total), ('vocab', 'dp'))  30.4 us
    dot_general x1, matrix products, per_device(): jnp.dot(hidden_states, head_weight, preferred_element_type=jnp.float32)  15.1 us
    dot_general x1, matrix products, per_device(): lax.dot_general(head_weight, logit_grad, (((1,), (1,)), ((), ())), prefer...  14.5 us
    dot_general x1, matrix products, per_device(): lax.dot_general(state_cols, lax.all_gather(logit_grad, 'teacher', axis=0,...  13.9 us
    all_to_all x1, waiting for transfers between devices, per_device(): lax.all_to_all(teacher_logits, 'teacher', split_axis=0, concat_axis=1, ti...  10.8 us
  transfers between devices with their start and end apart: 4, of which 3 were waited for; matrix products, arithmetic and copies ran while one was open for 11% of the time, Pallas kernels for 0%

commit v1 on v0

v1 whole, which is shorter than its diff:
```python
import functools

import jax
import jax.numpy as jnp
from jax import lax
from jax.experimental import pallas as pl
from jax.experimental.pallas import tpu as pltpu
from jax.sharding import PartitionSpec as P

MESH = pl.DeviceIdType.MESH
F32 = jnp.float32
BF16 = jnp.bfloat16
LANES = 128
CHUNKS = 4
ROWS = 32


def flip(v, mask):
    out = v
    bit = 1
    while bit <= mask:
        if mask & bit:
            out = out + bit * (1 - 2 * ((v // bit) % 2))
        bit *= 2
    return out


def low_bit(m):
    return m & (-m)


def aligned(start, size):
    return pl.ds(pl.multiple_of(start, size), size)


def kernel(nv, nd, nt, h_hbm, w_hbm, t_hbm, tw_ref, hid_ref, wg_hbm,
           W, H, Ho, S, T, G, Go, sb, rb, zs, zr, WA, stage, ST, stats,
           w_sem, h_sem, tl_sem, out_sem,
           tx_s, tx_r, hx_s, hx_r, hz_s, hz_r, hv_s, hv_r,
           st_s, st_r, gx_s, gx_r, rs_s, rs_r, z_s, z_r):
    v = lax.axis_index("vocab")
    d = lax.axis_index("dp")
    t = lax.axis_index("teacher")
    plane = nv * nd
    me = v * nd + d
    tok, D = H.shape
    vs = W.shape[1]
    vt = T.shape[2]
    dh = D // nt
    R = tok // plane
    dv = D // nv
    dz = dv // nd
    tc = tok // CHUNKS

    def plane_peer(k):
        p = (me + k) % plane
        return (p // nd, p % nd, t)

    def t_peer(k):
        return (v, d, (t + k) % nt)

    bar = pltpu.get_barrier_semaphore()
    for k in range(1, plane):
        pl.semaphore_signal(bar, inc=1, device_id=plane_peer(k), device_id_type=MESH)
    for k in range(1, nt):
        pl.semaphore_signal(bar, inc=1, device_id=t_peer(k), device_id_type=MESH)

    wn = w_sem.shape[0]
    hn = h_sem.shape[0]
    wc = vs // wn
    hc = tok // hn
    w_cp = [pltpu.make_async_copy(w_hbm.at[:, pl.ds(i * wc, wc)], W.at[:, pl.ds(i * wc, wc)], w_sem.at[i]) for i in range(wn)]
    h_cp = [pltpu.make_async_copy(h_hbm.at[pl.ds(i * hc, hc)], H.at[pl.ds(i * hc, hc)], h_sem.at[i]) for i in range(hn)]
    h_cp[0].start()
    w_cp[0].start()
    for i in range(1, wn):
        w_cp[i].start()
    for i in range(1, hn):
        h_cp[i].start()
    tl_cp = pltpu.make_async_copy(t_hbm.at[aligned(t * tok, tok)], T.at[t], tl_sem)
    tl_cp.start()
    pl.semaphore_wait(bar, plane + nt - 2)

    def remote(src, dst, ss, rs, dev):
        return pltpu.make_async_remote_copy(src_ref=src, dst_ref=dst, send_sem=ss, recv_sem=rs, device_id=dev, device_id_type=MESH)

    sent = []
    hx = []
    for k in range(1, nt):
        p = (t + k) % nt
        hx.append(remote(h_hbm.at[aligned(me * R, R), aligned(p * dh, dh)], Ho.at[k - 1, aligned(me * R, R)],
                         hx_s.at[k - 1], hx_r.at[k - 1], t_peer(k)))
        hx[-1].start()
    tx = []
    for k in range(1, nt):
        p = (t + k) % nt
        tx.append(remote(t_hbm.at[aligned(p * tok, tok)], T.at[t], tx_s.at[k - 1], tx_r.at[k - 1], t_peer(k)))
        tx[-1].start()
    sent += hx + tx

    def logits(i, j):
        def body(n, _):
            c = aligned(j * wc + n * 256, 256) if wc > 256 else pl.ds(j * wc, wc)
            S[pl.ds(i * hc, hc), c] = jnp.dot(H[pl.ds(i * hc, hc), :], W[:, c], preferred_element_type=F32)
            return 0
        lax.fori_loop(0, max(wc // 256, 1), body, 0)

    hz = []
    hv = []
    order = []
    bit = nv // 2
    held = [0]
    n = 0
    while bit >= 1:
        order.append((bit, [(m, n + i) for i, m in enumerate(held)]))
        n += len(held)
        held = held + [m + bit for m in held]
        bit //= 2

    def start_hz():
        for c in hx:
            c.wait_recv()
        for b in range(nt - 1):
            for k in range(1, nd):
                rows = aligned(me * R, R)
                i = b * (nd - 1) + k - 1
                hz.append(remote(Ho.at[b, rows], Ho.at[b, rows], hz_s.at[i], hz_r.at[i], (v, (d + k) % nd, t)))
                hz[-1].start()

    def start_hv(stage_i):
        bit, items = order[stage_i]
        out = []
        for b in range(nt - 1):
            for m, i in items:
                rows = aligned(flip(v, m) * (nd * R), nd * R)
                i = b * (nv - 1) + i
                out.append(remote(Ho.at[b, rows], Ho.at[b, rows], hv_s.at[i], hv_r.at[i], (flip(v, bit), d, t)))
                out[-1].start()
        hv.append(out)

    for i in range(hn):
        h_cp[i].wait()
        for j in range(wn):
            if i == 0:
                w_cp[j].wait()
            logits(i, j)
        if i == 0:
            start_hz()

    lane = lax.broadcasted_iota(jnp.int32, (ROWS, LANES), 1)

    def s_stats(n, _):
        r = aligned(n * ROWS, ROWS)
        s = S[r, :]
        m = jnp.max(s, axis=1, keepdims=True)
        e = jnp.exp(s - m)
        S[r, :] = e
        ST[r, :] = jnp.where(lane == 0, m, jnp.sum(e, axis=1, keepdims=True))
        return 0

    lax.fori_loop(0, tok // ROWS, s_stats, 0)

    tl_cp.wait()
    for c in tx:
        c.wait_recv()

    def t_stats(n, _):
        r = aligned(n * ROWS, ROWS)
        parts = [T[j, r, :].astype(F32) for j in range(nt)]
        m = functools.reduce(jnp.maximum, [jnp.max(x, axis=1, keepdims=True) for x in parts])
        l = functools.reduce(jnp.add, [jnp.sum(jnp.exp(x - m), axis=1, keepdims=True) for x in parts])
        ST[r, :] = jnp.where(lane < 2, ST[r, :], jnp.where(lane == 2, m, l))
        return 0

    lax.fori_loop(0, tok // ROWS, t_stats, 0)

    for j in range(tok // LANES):
        c = pl.ds(j * LANES, LANES)
        stats[0, :, c] = ST[c, :].T[0:8, :]

    st = []
    for k in range(1, plane):
        st.append(remote(stats.at[0], stats.at[k], st_s.at[k - 1], st_r.at[k - 1], plane_peer(k)))
        st[-1].start()
    sent += st

    for c in hz:
        c.wait_recv()
    start_hv(0)

    for c in st:
        c.wait_recv()

    tops = jnp.max(stats[...], axis=0)
    s_top = tops[0:1]
    t_top = tops[2:3]
    s_sum = jnp.sum(stats[:, 1, :] * jnp.exp(stats[:, 0, :] - s_top), axis=0, keepdims=True)
    t_sum = jnp.sum(stats[:, 3, :] * jnp.exp(stats[:, 2, :] - t_top), axis=0, keepdims=True)
    s_norm = s_top + jnp.log(s_sum)
    t_norm = t_top + jnp.log(t_sum)
    tw = tw_ref[...]
    fac = tw * jnp.exp(stats[0, 0:1, :] - s_norm)
    row = lax.broadcasted_iota(jnp.int32, (LANES, tok), 0)
    mat = jnp.where(row == 0, fac, jnp.where(row == 1, t_norm, tw))
    for j in range(tok // LANES):
        ST[j * LANES:(j + 1) * LANES, :] = mat[:, j * LANES:(j + 1) * LANES].T

    def make_grad(c):
        def body(n, _):
            r = aligned(c * tc + n * ROWS, ROWS)
            a = ST[r, 0:1]
            tn = ST[r, 1:2]
            w = ST[r, 2:3]
            for j in range(nt):
                cols = pl.ds(j * vt, vt)
                G[r, cols] = (S[r, cols] * a - w * jnp.exp(T[j, r, :].astype(F32) - tn)).astype(BF16)
            return 0
        lax.fori_loop(0, tc // ROWS, body, 0)

    gx = [[] for _ in range(CHUNKS)]

    def send_grad(c):
        r = pl.ds(c * tc, tc)
        for k in range(1, nt):
            i = (k - 1) * CHUNKS + c
            cp = remote(G.at[r], Go.at[k - 1, r], gx_s.at[i], gx_r.at[i], t_peer(k))
            cp.start()
            gx[c].append(cp)
            sent.append(cp)

    DT = min(dv, 512)

    def share(c, m, dst, adds):
        base = flip(v, m) * dv

        def body(n, _):
            r = aligned(n * DT, DT)
            p = lax.dot_general(W[aligned(base + n * DT, DT), :], G[pl.ds(c * tc, tc), :],
                                (((1,), (1,)), ((), ())), preferred_element_type=F32)
            for s in adds:
                p = p + rb[s - 1, c, r, :].astype(F32)
            dst[r, :] = p.astype(BF16)
            return 0
        lax.fori_loop(0, dv // DT, body, 0)

    rs = {}

    def send_share(c, m):
        low = low_bit(m)
        adds = []
        b = 1
        while b < low:
            adds.append(m ^ b)
            b *= 2
        for s in adds:
            rs[(c, s)].wait_recv()
        share(c, m, sb.at[m - 1, c], adds)
        i = (m - 1) * CHUNKS + c
        cp = remote(sb.at[m - 1, c], rb.at[m - 1, c], rs_s.at[i], rs_r.at[i], (flip(v, low), d, t))
        cp.start()
        rs[(c, m)] = cp
        sent.append(cp)

    first = [m for m in range(nv - 1, 0, -1) if low_bit(m) == 1]
    later = sorted([m for m in range(1, nv) if low_bit(m) > 1], key=lambda m: (low_bit(m), -m))

    zc = [[] for _ in range(CHUNKS)]

    def to_dp(c):
        adds = []
        b = 1
        while b < nv:
            adds.append(b)
            b *= 2
        for s in adds:
            rs[(c, s)].wait_recv()
        share(c, 0, zs.at[c], adds)
        for k in range(1, nd):
            i = (k - 1) * CHUNKS + c
            p = (d + k) % nd
            cp = remote(zs.at[c, aligned(p * dz, dz)], zr.at[k - 1, c], z_s.at[i], z_r.at[i], (v, p, t))
            cp.start()
            zc[c].append(cp)
            sent.append(cp)

    def finish(c):
        for cp in zc[c]:
            cp.wait_recv()
        x = zs[c, aligned(d * dz, dz), :].astype(F32)
        for k in range(1, nd):
            x = x + zr[k - 1, c].astype(F32)
        hid_ref[:, c * tc:(c + 1) * tc] = x.astype(BF16)

    wt = 256
    n_w = dh // wt

    def own_weight(i0, i1):
        def body(i, _):
            WA[aligned(i * wt, wt), :] = lax.dot_general(
                H[:, aligned(t * dh + i * wt, wt)], G[...], (((0,), (0,)), ((), ())), preferred_element_type=F32)
            return 0
        lax.fori_loop(i0, i1, body, 0)

    def part_a(c):
        make_grad(c)
        send_grad(c)
        for m in first:
            send_share(c, m)

    def part_b(c):
        for m in later:
            send_share(c, m)

    part_a(0)
    for c in range(1, CHUNKS):
        part_a(c)
        part_b(c - 1)
    part_b(CHUNKS - 1)
    sent += hz
    for c in hv[0]:
        c.wait_recv()
    for s in range(1, len(order)):
        start_hv(s)
        if s < len(order) - 1:
            for c in hv[s]:
                c.wait_recv()
    for c in range(CHUNKS):
        own_weight(c * n_w // CHUNKS, (c + 1) * n_w // CHUNKS)
        to_dp(c)
    for out in hv[1:][-1:]:
        for c in out:
            c.wait_recv()
    for out in hv:
        sent += out
    for c in range(CHUNKS):
        for cp in gx[c]:
            cp.wait_recv()

    def out_copy(i, slot):
        return pltpu.make_async_copy(stage.at[slot], wg_hbm.at[aligned(i * wt, wt)], out_sem.at[slot])

    def last_weight(i, _):
        slot = i % 2

        @pl.when(i >= 2)
        def _():
            out_copy(i - 2, slot).wait()
        x = WA[aligned(i * wt, wt), :]
        for b in range(nt - 1):
            x = x + lax.dot_general(Ho[b, :, aligned(i * wt, wt)], Go[b], (((0,), (0,)), ((), ())), preferred_element_type=F32)
        stage[slot] = x.astype(BF16)
        out_copy(i, slot).start()
        return 0

    lax.fori_loop(0, n_w, last_weight, 0)
    for c in range(CHUNKS):
        finish(c)
    for i in range(n_w - 2, n_w):
        out_copy(i, i % 2).wait()
    for cp in sent:
        cp.wait_send()


def per_device(nv, nd, nt, hidden_states, head_weight, teacher_logits, token_weight):
    tok, D = hidden_states.shape
    vs = head_weight.shape[1]
    vt = teacher_logits.shape[1]
    plane = nv * nd
    dv = D // nv
    dz = dv // nd
    dh = D // nt
    tc = tok // CHUNKS
    dma = lambda n: pltpu.SemaphoreType.DMA((n,))
    scratch = [
        pltpu.VMEM((D, vs), BF16),
        pltpu.VMEM((tok, D), BF16),
        pltpu.VMEM((nt - 1, tok, dh), BF16),
        pltpu.VMEM((tok, vs), F32),
        pltpu.VMEM((nt, tok, vt), BF16),
        pltpu.VMEM((tok, vs), BF16),
        pltpu.VMEM((nt - 1, tok, vs), BF16),
        pltpu.VMEM((nv - 1, CHUNKS, dv, tc), BF16),
        pltpu.VMEM((nv - 1, CHUNKS, dv, tc), BF16),
        pltpu.VMEM((CHUNKS, dv, tc), BF16),
        pltpu.VMEM((nd - 1, CHUNKS, dz, tc), BF16),
        pltpu.VMEM((dh, vs), F32),
        pltpu.VMEM((2, 256, vs), BF16),
        pltpu.VMEM((tok, LANES), F32),
        pltpu.VMEM((plane, 8, tok), F32),
        dma(4), dma(2), pltpu.SemaphoreType.DMA, dma(2),
        dma(nt - 1), dma(nt - 1), dma(nt - 1), dma(nt - 1),
        dma((nt - 1) * (nd - 1)), dma((nt - 1) * (nd - 1)),
        dma((nt - 1) * (nv - 1)), dma((nt - 1) * (nv - 1)),
        dma(plane - 1), dma(plane - 1),
        dma((nt - 1) * CHUNKS), dma((nt - 1) * CHUNKS),
        dma((nv - 1) * CHUNKS), dma((nv - 1) * CHUNKS),
        dma((nd - 1) * CHUNKS), dma((nd - 1) * CHUNKS),
    ]
    any_spec = pl.BlockSpec(memory_space=pl.ANY)
    vmem_spec = pl.BlockSpec(memory_space=pltpu.VMEM)
    hid, wg = pl.pallas_call(
        functools.partial(kernel, nv, nd, nt),
        out_shape=(jax.ShapeDtypeStruct((dz, tok), BF16), jax.ShapeDtypeStruct((dh, vs), BF16)),
        in_specs=[any_spec, any_spec, any_spec, vmem_spec],
        out_specs=(vmem_spec, any_spec),
        scratch_shapes=scratch,
        compiler_params=pltpu.CompilerParams(
            collective_id=0, has_side_effects=True, vmem_limit_bytes=62 * 1024 * 1024),
    )(hidden_states, head_weight, teacher_logits, token_weight.reshape(1, tok))
    return hid.T, wg


def solution(mesh):
    sizes = mesh.shape
    return jax.shard_map(
        functools.partial(per_device, sizes["vocab"], sizes["dp"], sizes["teacher"]),
        mesh=mesh,
        in_specs=(
            P("teacher", None),
            P(None, ("vocab", "dp")),
            P(None, ("vocab", "dp", "teacher")),
            P("teacher"),
        ),
        out_specs=(P("teacher", ("vocab", "dp")), P("teacher", ("vocab", "dp"))),
        check_vma=False,
    )
```

time: 394 us -> 138 us (0.35)
  waiting for transfers between devices: 251 us -> 0 us
  Pallas kernels: 0 us -> 129 us
  blocking collectives: 64.3 us -> 0 us
  matrix products: 43.5 us -> 0 us
  between operations: 15.5 us -> 0.64 us
  other arithmetic: 10.8 us -> 0 us
  starting transfers between devices: 4.47 us -> 0 us
    all_gather x2 -> x0, waiting for transfers between devices: 239 us -> none  [the longest x1 200 us: per_device(): lax.all_gather(hidden_states, 'teacher', axis=0, tiled=True)]
    pallas_call x0 -> x1, Pallas kernels: none -> 129 us  [per_device(): pl.pallas_call(functools.partial(kernel, nv, nd, nt), out_shape=(jax.Shap...]
    dot_general x3 -> x0, matrix products: 43.5 us -> none  [the longest x1 15.1 us: per_device(): jnp.dot(hidden_states, head_weight, preferred_element_type=jnp.float32)]
    pmax x1 -> x0, blocking collectives: 33.9 us -> none  [per_device(): lax.pmax((student_top, teacher_top), ('vocab', 'dp'))]
    psum x1 -> x0, blocking collectives: 30.4 us -> none  [per_device(): lax.psum((student_total, teacher_total), ('vocab', 'dp'))]
    all_to_all x1 -> x0, waiting for transfers between devices: 10.8 us -> none  [per_device(): lax.all_to_all(teacher_logits, 'teacher', split_axis=0, concat_axis=1, ti...]
    convert_element_type x2 -> x0, other arithmetic: 6.85 us -> none  [the longest x1 4.78 us: per_device(): logit_grad = (token_weight[:, None] * (jnp.exp(logits - student_norm[:, N...]
    unnamed x4 -> x2, local copies, waits for them, and re-layouts: 0.6 us -> 6.68 us
  transfers between devices with their start and end apart: 4 -> 0, of which waited for: 3 -> 0; matrix products, arithmetic and copies ran while one was open for 11% -> 0% of each run, Pallas kernels for 0% -> 0%
where the time goes in v1:
time: 138 us; the launch traced here: 137 us
  Pallas kernels  129 us (93%)
  local copies, waits for them, and re-layouts  6.68 us (5%)
    pallas_call x1, Pallas kernels, per_device(): pl.pallas_call(functools.partial(kernel, nv, nd, nt), out_shape=(jax.Shap...  129 us
    unnamed x2, local copies, waits for them, and re-layouts  6.68 us

profile of v1, /device:TPU:0, one launch (start us, length us, event | category | flops | bytes accessed | tf_op | source)
XLA Modules:
  0.0 136.8 jit_solution(6076098196609828218)
XLA Ops:
  0.6 129.5 %shard_map.59 = (bf16[256,1024]{1,0:T(8,128)(2,1)}, bf16[2048,1024]{1,0:T(8,128)(2,1)}) custom-call(bf16[1024,4096]{1,0:T(8,128)(2,1)} %h_hbm.1, bf16[4096,1024]{1,0:T(8,128)(2,1)} %w_hbm.1, bf16[2048,512]{1,0:T(8,128)(2,1)} %t_hbm.1, f32[1,1024]{1,0:T(1,128)} %bitcast.3), custom_call_target="tpu_custom_call" | custom-call | tf_op jit(solution)/shard_map/pallas_call | solution.py:401
  130.1 2.0 %copy.6 = bf16[1024,256]{1,0:T(8,128)(2,1)} copy(bf16[1024,256]{0,1:T(8,128)(2,1)} %bitcast.2) | data formatting | bytes 1048576
  132.2 4.6 %copy.8 = bf16[2048,1024]{1,0:T(8,128)(2,1)} copy(bf16[2048,1024]{1,0:T(8,128)(2,1)} %get-tuple-element.11) | data formatting | bytes 8388608
